TPU v7x, 32 devices: a whole 2x2x4 slice. The times are simulated.
32 devices in a mesh: groups: 2 (over y), tp: 4 (over x, core), sub: 4 (over z).
Axes of the slice: x: 2, y: 2, z: 4, core: 2. Of those that a mesh axis runs over, the one named last changes fastest.
Arguments:
- gate_pre: bfloat16 [1536, 32768], P('groups', ('tp', 'sub')), parts along dimension 0, may hold values from -8 to 8
- up_pre: bfloat16 [1536, 32768], P('groups', ('tp', 'sub')), parts along dimension 0, may hold values from -8 to 8
- down_weight: bfloat16 [32768, 16384], P('tp', 'sub'), may hold values from -0.046875 to 0.046875
- residual: bfloat16 [1536, 16384], P('groups', ('sub', 'tp')), parts along dimension 0, may hold values from -20 to 20
- signs: int32 [16384], P('sub'), may hold values from -1 to 1, as said below
- row_slot: int32 [1536], P('groups'), parts along dimension 0, may hold values from 0 to 767, each once
- norm_gain: float32 [16384], P('sub'), may hold values from 0.1 to 1.9
Outputs:
- stream: bfloat16 [1536, 16384], P('groups', ('sub', 'tp')), parts along dimension 0
- normed: bfloat16 [1536, 16384], P('groups', 'sub'), parts along dimension 0
There are 2 independent parts, one for each index of `groups`. A program takes and returns all parts, laid end to end along the dimension named above; an argument that names none is the same for every part. Nothing has to cross between parts.
Inputs may be any that keep to these rules, and one draw needn't show every extreme that they name: `row_slot`: a permutation of the slots. `signs`: every entry is -1 or 1.
All inputs are finite; a program needn't handle non-finite values.
Results may differ from a plain program's by a relative error of at most 0.0056.
Values may be sent and summed in bfloat16 or wider, within the bound.
No kernel may reach another device: no remote copies, remote signals or barrier semaphores. Data moves between devices by JAX's collectives and lax.ppermute only.
A program may use at most 256 MiB of HBM per device.

v0:
```python
import jax
import jax.numpy as jnp
from jax import lax
from jax.sharding import PartitionSpec as P

D = 16384


def hadamard():
    index = jnp.arange(128, dtype=jnp.int32)
    common = index[:, None] & index[None, :]
    parity = sum((common >> shift & 1 for shift in range(7)))
    return jnp.where(parity % 2 == 0, 1.0, -1.0).astype(jnp.float32) * 0.08838834764831845


def shards(gate_pre, up_pre, down_weight, residual, signs, row_slot, norm_gain):
    hidden = (jax.nn.silu(gate_pre.astype(jnp.float32)) * up_pre.astype(jnp.float32)).astype(
        jnp.bfloat16
    )
    batch = hidden.shape[0]
    columns = down_weight.shape[1]
    gathered = lax.all_gather(hidden, "sub", axis=1, tiled=True)
    partial_value = jnp.dot(gathered, down_weight, preferred_element_type=jnp.float32)
    parts_tp = lax.axis_size("tp")
    blocks_own = columns // (parts_tp * 128)
    width = blocks_own * 128
    matrix = hadamard()
    sign_blocks = signs.astype(jnp.float32).reshape(columns // 128, 128)
    signed = partial_value.reshape(batch, columns // 128, 128) * sign_blocks
    rotated = jnp.einsum("rbk,kj->rbj", signed, matrix, precision=lax.Precision.HIGHEST)
    rotated = rotated.reshape(batch, parts_tp, width)
    received = lax.all_to_all(rotated, "tp", split_axis=1, concat_axis=1, tiled=True)
    delta = jnp.sum(received, axis=1)
    mine = jnp.take(residual, row_slot, axis=0)
    stream = (mine.astype(jnp.float32) + delta).astype(jnp.bfloat16)
    local = stream.astype(jnp.float32)
    squares = lax.psum(jnp.sum(local * local, axis=1), ("tp", "sub"))
    inverse = lax.rsqrt(squares / D + 1e-05)
    gain_own = lax.dynamic_slice_in_dim(norm_gain, lax.axis_index("tp") * width, width, 0)
    normed_own = (local * inverse[:, None] * gain_own).astype(jnp.bfloat16)
    normed = lax.all_gather(normed_own, "tp", axis=1, tiled=True)
    return (stream, normed)


def solution(mesh):
    return jax.shard_map(
        shards,
        mesh=mesh,
        in_specs=(
            P("groups", ("tp", "sub")),
            P("groups", ("tp", "sub")),
            P("tp", "sub"),
            P("groups", ("sub", "tp")),
            P("sub"),
            P("groups"),
            P("sub"),
        ),
        out_specs=(P("groups", ("sub", "tp")), P("groups", "sub")),
        check_vma=False,
    )
```

profile of v0, /device:TPU:0, one launch (start us, length us, event | category | flops | bytes accessed | tf_op | source)
XLA Modules:
  0.0 556.0 jit_solution(11066943557258601212)
XLA Ops:
  7.2 0.0 copy-start
  7.2 0.0 all-gather.3.cloned.1.call-start
  7.2 5.2 fusion.7
  12.4 0.0 copy-start.3
  12.5 0.0 all-gather.3.cloned.1.call-update
  12.5 0.7 copy-done.3
  13.2 220.4 %all-gather.3.cloned.1.call-done = bf16[768,8192]{1,0:T(8,128)(2,1)} async-done(((bf16[768,2048]{1,0:T(8,128)(2,1)}), bf16[768,8192]{1,0:T(8,128)(2,1)}) %all-gather.3.cloned.1.call-update) | async-done | bytes 12582928 | tf_op jit(solution)/shard_map/all_gather | solution.py:22
  233.5 58.9 %convolution_bitcast_fusion = f32[96,32,8,128]{3,2,1,0:T(8,128)S(1)} fusion(bf16[768,8192]{1,0:T(8,128)(2,1)} %all-gather.3.cloned.1.call-done, bf16[8192,4096]{1,0:T(8,128)(2,1)} %param.9), kind=kOutput, calls=%fused_computation.12 | convolution fusion | flops 51539607552 | bytes 92274688 | tf_op jit(solution)/shard_map/dot_general | solution.py:23
  292.4 14.8 %fusion = f32[768,32,128]{0,2,1:T(8,128)} fusion(f32[96,32,8,128]{3,2,1,0:T(8,128)S(1)} %convolution_bitcast_fusion, f32[32,128]{1,0:T(8,128)S(1)} %convert_bitcast_fusion), kind=kOutput, calls=%fused_computation.2 | convolution fusion | flops 4835557376 | bytes 25182208 | tf_op jit(solution)/shard_map/rbk,kj->rbj/dot_general | solution.py:30
  307.3 0.0 copy-start.2
  307.3 6.6 %all-to-all-start = ((f32[768,4,1024]{0,2,1:T(8,128)}), f32[768,4,1024]{0,2,1:T(8,128)}, u32[]{:S(2)}, u32[]{:S(2)}) async-start(f32[768,4,1024]{0,2,1:T(8,128)} %bitcast.13), calls=%async_computation | async-start | bytes 25165824 | tf_op jit(solution)/shard_map/all_to_all | solution.py:32
  313.9 0.0 all-gather.5.cloned.1.call-start
  313.9 0.0 copy-done.2
  314.0 0.0 copy-done
  314.0 3.6 gather_fusion
  317.6 134.4 %all-to-all-done = f32[768,4,1024]{0,2,1:T(8,128)} async-done(((f32[768,4,1024]{0,2,1:T(8,128)}), f32[768,4,1024]{0,2,1:T(8,128)}, u32[]{:S(2)}, u32[]{:S(2)}) %all-to-all-start) | async-done | bytes 12582944 | tf_op jit(solution)/shard_map/all_to_all | solution.py:32
  452.0 7.5 %reduce_sum.18 = f32[768,1024]{0,1:T(8,128)} reduce(f32[768,4,1024]{0,2,1:T(8,128)} %all-to-all-done, f32[]{:T(128)} %constant.59.clone.1), dimensions={1}, to_apply=%region_0.1 | reduce | flops 2359296 | bytes 15728644 | tf_op jit(solution)/shard_map/reduce_sum | solution.py:33
  459.5 3.5 copy.11
  463.0 0.0 dynamic-slice-start
  463.0 3.1 fusion.8
  466.1 0.0 copy-start.1
  466.2 29.7 %psum.7 = f32[768]{0:T(1024)S(1)} all-reduce(f32[768]{0:T(1024)S(1)} %get-tuple-element.2), channel_id=1, replica_groups=mesh['groups'=2,'tp'=4,'sub'=4] {'tp','sub'}, use_global_device_ids=true, to_apply=%region_2.3 | all-reduce | flops 768 | bytes 6144 | tf_op jit(solution)/shard_map/psum | solution.py:37
  495.9 0.0 dynamic-slice-done
  495.9 1.6 fusion.10
  497.4 0.0 all-gather.5.cloned.1.call-update
  497.5 45.4 %all-gather.5.cloned.1.call-done = bf16[768,4096]{1,0:T(8,128)(2,1)} async-done(((bf16[768,1024]{1,0:T(8,128)(2,1)}), bf16[768,4096]{1,0:T(8,128)(2,1)}) %all-gather.5.cloned.1.call-update) | async-done | bytes 6291472 | tf_op jit(solution)/shard_map/all_gather | solution.py:41
  542.9 6.3 %copy.18 = bf16[768,4096]{1,0:T(8,128)(2,1)} copy(bf16[768,4096]{1,0:T(8,128)(2,1)} %all-gather.5.cloned.1.call-done) | data formatting | bytes 12582912
  549.2 0.0 copy-done.1
  (5 shorter events, 0.0 us)
Async XLA Ops:
  7.2 306.8 %copy-start = (bf16[768,1024]{1,0:T(8,128)(2,1)S(1)}, bf16[768,1024]{1,0:T(8,128)(2,1)}, u32[]{:S(2)}) copy-start(bf16[768,1024]{1,0:T(8,128)(2,1)} %param.10) | copy-start | bytes 4718596
  7.2 226.4 %all-gather.3.cloned.1.call-start = ((), (), s32[]{:S(2)}) async-start(), calls=%async_computation.1 | async-start | bytes 15728640 | tf_op jit(solution)/shard_map/all_gather | solution.py:22
  12.4 0.7 copy-start.3
  307.3 6.7 %copy-start.2 = (s32[768]{0:T(1024)S(1)}, s32[768]{0:T(1024)}, u32[]{:S(2)}) copy-start(s32[768]{0:T(1024)} %param.12) | copy-start | bytes 9220
  307.3 144.8 %all-to-all-start = ((f32[768,4,1024]{0,2,1:T(8,128)}), f32[768,4,1024]{0,2,1:T(8,128)}, u32[]{:S(2)}, u32[]{:S(2)}) async-start(f32[768,4,1024]{0,2,1:T(8,128)} %bitcast.13), calls=%async_computation | async-start | bytes 25165824 | tf_op jit(solution)/shard_map/all_to_all | solution.py:32
  313.9 229.0 %all-gather.5.cloned.1.call-start = ((), (), s32[]{:S(2)}) async-start(), calls=%async_computation.2 | async-start | bytes 7864320 | tf_op jit(solution)/shard_map/all_gather | solution.py:41
  463.0 32.9 %dynamic-slice-start = ((f32[4096]{0:T(1024)}, s32[]{:T(128)}), f32[1024]{0:T(1024)S(1)}, s32[]{:S(2)}) async-start(f32[4096]{0:T(1024)} %param.13, s32[]{:T(128)} %select_n.27), calls=%async_computation.3 | async-start | bytes 8704 | tf_op jit(solution)/shard_map/dynamic_slice | solution.py:39
  466.1 83.0 %copy-start.1 = (bf16[768,1024]{1,0:T(8,128)(2,1)}, bf16[768,1024]{1,0:T(8,128)(2,1)S(1)}, u32[]{:S(2)}) copy-start(bf16[768,1024]{1,0:T(8,128)(2,1)S(1)} %get-tuple-element.6) | copy-start | bytes 4718596
Sparse Core Ops, SparseCore 0:
  12.6 220.8 all-gather.2
  497.6 45.2 all-gather.4
where the time goes:
time: 556 us
  waiting for transfers between devices  400 us (72%)
  matrix products  73.7 us (13%)
  blocking collectives  29.7 us (5%)
  other arithmetic  17.4 us (3%)
  local copies, waits for them, and re-layouts  14.1 us (3%)
  between operations  14.1 us (3%)
  starting transfers between devices  6.71 us (1%)
    all_gather x1, waiting for transfers between devices, shards(): gathered = lax.all_gather(hidden, 'sub', axis=1, tiled=True)  220 us
    all_to_all x1, waiting for transfers between devices, shards(): lax.all_to_all(rotated, 'tp', split_axis=1, concat_axis=1, tiled=True)  134 us
    dot_general x1, matrix products, shards(): jnp.dot(gathered, down_weight, preferred_element_type=jnp.float32)  58.9 us
    all_gather x1, waiting for transfers between devices, shards(): normed = lax.all_gather(normed_own, 'tp', axis=1, tiled=True)  45.4 us
    psum x1, blocking collectives, shards(): squares = lax.psum(jnp.sum(local * local, axis=1), ('tp', 'sub'))  29.7 us
    dot_general x1, matrix products, shards(): jnp.einsum('rbk,kj->rbj', signed, matrix, precision=lax.Precision.HIGHEST)  14.8 us
  transfers between devices with their start and end apart: 3, of which 3 were waited for; matrix products, arithmetic and copies ran while one was open for 1% of the time, Pallas kernels for 0%

commit v1 on v0

v1 whole, which is shorter than its diff:
```python
import functools

import jax
import jax.numpy as jnp
from jax import lax
from jax.experimental import pallas as pl
from jax.experimental.pallas import tpu as pltpu
from jax.sharding import PartitionSpec as P

D = 16384
H_SCALE = 0.08838834764831845
VMEM = 48 * 1024 * 1024
TOKEN = (8, 128)


def hadamard_signs():
    index = jnp.arange(128, dtype=jnp.int32)
    common = index[:, None] & index[None, :]
    parity = sum((common >> shift & 1 for shift in range(7)))
    return jnp.where(parity % 2 == 0, 1.0, -1.0).astype(jnp.bfloat16)


def row_chunks(rows, tp):
    if tp == 4 and rows == 768:
        return [128] * 6
    return [rows // 2] * 2


def block_of(width, most):
    size = min(width, most)
    while width % size:
        size //= 2
    return size


def hidden_kernel(more, gate, up, *refs):
    out, token = refs[more:]
    value = gate[...].astype(jnp.float32)
    value = value / (1.0 + jnp.exp(-value)) * up[...].astype(jnp.float32)
    out[...] = value.astype(jnp.bfloat16)
    token[...] = jnp.zeros(TOKEN, jnp.float32)


def hidden_chunk(gate, up, start, rows, after):
    columns = gate.shape[1]
    place = start // rows
    line = pl.BlockSpec((rows, columns), lambda i: (place, 0))
    small = pl.BlockSpec(TOKEN, lambda i: (0, 0))
    return pl.pallas_call(
        functools.partial(hidden_kernel, len(after)),
        grid=(1,),
        in_specs=[line, line] + [small] * len(after),
        out_specs=[pl.BlockSpec((rows, columns), lambda i: (0, 0)), small],
        out_shape=[
            jax.ShapeDtypeStruct((rows, columns), jnp.bfloat16),
            jax.ShapeDtypeStruct(TOKEN, jnp.float32),
        ],
        compiler_params=pltpu.CompilerParams(vmem_limit_bytes=VMEM),
        name="hidden_chunk",
    )(gate, up, *after)


def matmul_kernel(tp, after, where, piece, weight, *refs):
    outs = refs[after : after + tp]
    token, total = refs[after + tp :]
    step = pl.program_id(0)
    me = where[1]
    width = total.shape[2]
    value = piece[...]
    for t in range(tp):
        product = jnp.dot(
            value, weight[:, t * width : (t + 1) * width], preferred_element_type=jnp.float32
        )

        @pl.when(step == 0)
        def _():
            total[t] = product

        @pl.when(step != 0)
        def _():
            total[t] += product

    @pl.when(step == pl.num_programs(0) - 1)
    def _():
        for d in range(tp):
            outs[d][...] = total[me ^ d].astype(outs[d].dtype)
        token[...] = jnp.zeros(TOKEN, jnp.float32)


def matmul_chunk(where, gathered, weight, tp, parts, after, arrived):
    rows = gathered.shape[0] // parts
    depth = gathered.shape[1]
    block = block_of(depth, 512)
    per = depth // block
    columns = weight.shape[1]
    width = columns // tp
    whole = pl.BlockSpec((rows, width), lambda j, s: (0, 0))
    return pl.pallas_call(
        functools.partial(matmul_kernel, tp, len(after) + len(arrived)),
        grid_spec=pltpu.PrefetchScalarGridSpec(
            num_scalar_prefetch=1,
            grid=(parts * per,),
            in_specs=[
                pl.BlockSpec((rows, block), lambda j, s: (j // per, j % per)),
                pl.BlockSpec((block, columns), lambda j, s: (j, 0)),
            ]
            + [pl.BlockSpec(TOKEN, lambda j, s: (0, 0))] * len(after)
            + [pl.BlockSpec(memory_space=pl.ANY)] * len(arrived),
            out_specs=[whole] * tp + [pl.BlockSpec(TOKEN, lambda j, s: (0, 0))],
            scratch_shapes=[pltpu.VMEM((tp, rows, width), jnp.float32)],
        ),
        out_shape=[jax.ShapeDtypeStruct((rows, width), jnp.float32)]
        + [jax.ShapeDtypeStruct((rows, width), jnp.bfloat16)] * (tp - 1)
        + [jax.ShapeDtypeStruct(TOKEN, jnp.float32)],
        compiler_params=pltpu.CompilerParams(vmem_limit_bytes=VMEM),
        cost_estimate=pl.CostEstimate(
            flops=2 * rows * parts * depth * columns,
            bytes_accessed=2 * weight.size,
            transcendentals=0,
        ),
        name="matmul_chunk",
    )(where, gathered, weight, *after, *arrived)


def stream_kernel(tp, more, *refs):
    own = refs[0]
    others = refs[1:tp]
    signs, matrix, residual = refs[tp : tp + 3]
    stream, chunk, squares = refs[tp + 3 + more :]
    total = own[...]
    for other in others:
        total = total + other[...].astype(jnp.float32)
    total = total * signs[...].astype(jnp.float32)
    rows, width = total.shape
    turn = matrix[...]
    for b in range(width // 128):
        piece = total[:, b * 128 : (b + 1) * 128]
        rotated = jnp.zeros((rows, 128), jnp.float32)
        for _ in range(3):
            part = piece.astype(jnp.bfloat16)
            rotated = rotated + jnp.dot(part, turn, preferred_element_type=jnp.float32)
            piece = piece - part.astype(jnp.float32)
        kept = residual[:, b * 128 : (b + 1) * 128].astype(jnp.float32)
        value = (kept + rotated * H_SCALE).astype(jnp.bfloat16)
        stream[:, b * 128 : (b + 1) * 128] = value
        chunk[:, b * 128 : (b + 1) * 128] = value
    local = chunk[...].astype(jnp.float32)
    squares[...] = lax.dot_general(
        jnp.ones((8, width), jnp.float32),
        local * local,
        (((1,), (1,)), ((), ())),
        precision=lax.Precision.HIGHEST,
        preferred_element_type=jnp.float32,
    )


def stream_chunk(pieces, signs, matrix, residual, so_far, start, after):
    tp = len(pieces)
    rows, width = pieces[0].shape
    place = start // rows
    vm = pl.BlockSpec((rows, width), lambda i: (0, 0))
    line = pl.BlockSpec((rows, width), lambda i: (place, 0))
    operands = [*pieces, signs, matrix, residual]
    specs = (
        [vm] * tp
        + [
            pl.BlockSpec((1, width), lambda i: (0, 0)),
            pl.BlockSpec((128, 128), lambda i: (0, 0)),
            line,
        ]
    )
    aliases = {}
    if so_far is not None:
        aliases = {len(operands): 0}
        operands.append(so_far)
        specs.append(pl.BlockSpec(memory_space=pl.ANY))
    operands += after
    specs += [pl.BlockSpec(TOKEN, lambda i: (0, 0))] * len(after)
    return pl.pallas_call(
        functools.partial(stream_kernel, tp, len(aliases) + len(after)),
        grid=(1,),
        in_specs=specs,
        out_specs=[line, vm, pl.BlockSpec((8, rows), lambda i: (0, 0))],
        out_shape=[
            jax.ShapeDtypeStruct(residual.shape, jnp.bfloat16),
            jax.ShapeDtypeStruct((rows, width), jnp.bfloat16),
            jax.ShapeDtypeStruct((8, rows), jnp.float32),
        ],
        input_output_aliases=aliases,
        compiler_params=pltpu.CompilerParams(vmem_limit_bytes=VMEM),
        name="stream_chunk",
    )(*operands)


def norm_kernel(tp, more, where, *refs):
    pieces = refs[:tp]
    squares = refs[tp : 2 * tp]
    gain = refs[2 * tp]
    out, token = refs[2 * tp + 1 + more :]
    token[...] = jnp.zeros(TOKEN, jnp.float32)
    me = where[1]
    total = squares[0][...]
    for other in squares[1:]:
        total = total + other[...]
    inverse = lax.rsqrt(total / D + 1e-05)
    scale = jnp.transpose(inverse)[:, 0:1]
    width = pieces[0].shape[1]
    for d in range(tp):
        at = pl.ds(pl.multiple_of((me ^ d) * width, width), width)
        value = pieces[d][...].astype(jnp.float32) * scale * gain[:, at]
        out[:, at] = value.astype(jnp.bfloat16)


def norm_chunk(where, pieces, squares, gain, so_far, start, all_rows, after):
    tp = len(pieces)
    rows, width = pieces[0].shape
    place = start // rows
    vm = pl.BlockSpec((rows, width), lambda i, s: (0, 0))
    operands = [*pieces, *squares, gain]
    specs = (
        [vm] * tp
        + [pl.BlockSpec((8, rows), lambda i, s: (0, 0))] * tp
        + [pl.BlockSpec((1, tp * width), lambda i, s: (0, 0))]
    )
    aliases = {}
    if so_far is not None:
        aliases = {1 + len(operands): 0}
        operands.append(so_far)
        specs.append(pl.BlockSpec(memory_space=pl.ANY))
    operands += after
    specs += [pl.BlockSpec(TOKEN, lambda i, s: (0, 0))] * len(after)
    return pl.pallas_call(
        functools.partial(norm_kernel, tp, len(aliases) + len(after)),
        grid_spec=pltpu.PrefetchScalarGridSpec(
            num_scalar_prefetch=1,
            grid=(1,),
            in_specs=specs,
            out_specs=[
                pl.BlockSpec((rows, tp * width), lambda i, s: (place, 0)),
                pl.BlockSpec(TOKEN, lambda i, s: (0, 0)),
            ],
        ),
        out_shape=[
            jax.ShapeDtypeStruct((all_rows, tp * width), jnp.bfloat16),
            jax.ShapeDtypeStruct(TOKEN, jnp.float32),
        ],
        input_output_aliases=aliases,
        compiler_params=pltpu.CompilerParams(vmem_limit_bytes=VMEM),
        name="norm_chunk",
    )(where, *operands)


def shards(sub, tp, gate_pre, up_pre, down_weight, residual, signs, row_slot, norm_gain):
    rows = gate_pre.shape[0]
    width = residual.shape[1]
    place = lax.axis_index("sub").astype(jnp.int32)
    me = lax.axis_index("tp").astype(jnp.int32)
    where = jnp.stack([place, me])
    matrix = hadamard_signs()
    mine = jnp.take(residual, row_slot, axis=0, mode="clip")
    signs_own = lax.dynamic_slice_in_dim(signs, me * width, width, 0).reshape(1, width)
    gain = norm_gain.reshape(1, -1)

    def swap(value, d):
        return lax.ppermute(value, "tp", [(i, i ^ d) for i in range(tp)])

    sizes = row_chunks(rows, tp)
    starts = [sum(sizes[:c]) for c in range(len(sizes))]
    last = len(sizes) - 1
    gathered = []
    after = []
    for start, size in zip(starts, sizes):
        own, token = hidden_chunk(gate_pre, up_pre, start, size, after)
        gathered.append(lax.all_gather(own, "sub", axis=0, tiled=True))
        after = [token]
    stream = normed = None
    chunks, squares = [], []

    def exchange(local):
        along = local
        for d in range(1, sub):
            along = along + lax.ppermute(local, "sub", [(i, (i + d) % sub) for i in range(sub)])
        return [along] + [swap(along, d) for d in range(1, tp)]

    def normalise(group, totals, normed, after):
        for c in group:
            at = starts[c] - starts[group[0]]
            part = [t[:, at : at + sizes[c]] for t in totals]
            normed, token = norm_chunk(
                where, chunks[c], part, gain, normed, starts[c], rows, after
            )
            after = [token]
        return normed, after

    early = list(range(last))
    for c in range(len(sizes)):
        if c == last:
            totals = exchange(jnp.concatenate(squares, axis=1))
        arrived = chunks[c - 2][1:] if c >= 2 else []
        *sums, token = matmul_chunk(where, gathered[c], down_weight, tp, sub, after, arrived)
        after = [token]
        pieces = [sums[0]] + [swap(sums[d], d) for d in range(1, tp)]
        if c == last:
            normed, after = normalise(early, totals, normed, after)
        stream, chunk, local = stream_chunk(
            pieces, signs_own, matrix, mine, stream, starts[c], after
        )
        after = [local]
        chunks.append([chunk] + [swap(chunk, d) for d in range(1, tp)])
        squares.append(local)
    normed, _ = normalise([last], exchange(local), normed, [])
    return (stream, normed)


def solution(mesh):
    return jax.shard_map(
        functools.partial(shards, mesh.shape["sub"], mesh.shape["tp"]),
        mesh=mesh,
        in_specs=(
            P("groups", ("tp", "sub")),
            P("groups", ("tp", "sub")),
            P("tp", "sub"),
            P("groups", ("sub", "tp")),
            P("sub"),
            P("groups"),
            P("sub"),
        ),
        out_specs=(P("groups", ("sub", "tp")), P("groups", "sub")),
        check_vma=False,
    )
```

time: 556 us -> 447 us (0.80)
  waiting for transfers between devices: 400 us -> 124 us
  Pallas kernels: 0 us -> 234 us
  matrix products: 73.7 us -> 0 us
  blocking collectives: 29.7 us -> 0 us
  starting transfers between devices: 6.71 us -> 34.5 us
  local copies, waits for them, and re-layouts: 14.1 us -> 36.5 us
  other arithmetic: 17.4 us -> 0.18 us
    all_gather x2 -> x6, waiting for transfers between devices: 266 us -> 27.8 us  [shards(): gathered.append(lax.all_gather(own, 'sub', axis=0, tiled=True))]
    pallas_call x0 -> x24, Pallas kernels: none -> 234 us  [the longest x6 196 us: matmul_chunk(): pl.pallas_call(functools.partial(matmul_kernel, tp, len(after) + len(arri...]
    all_to_all x1 -> x0, waiting for transfers between devices: 134 us -> none  [shards(): lax.all_to_all(rotated, 'tp', split_axis=1, concat_axis=1, tiled=True)]
    ppermute x0 -> x48, waiting for transfers between devices: none -> 96.2 us  [the longest x42 88.8 us: swap(): return lax.ppermute(value, 'tp', [(i, i ^ d) for i in range(tp)])]
    dot_general x2 -> x0, matrix products: 73.7 us -> none  [the longest x1 58.9 us: shards(): jnp.dot(gathered, down_weight, preferred_element_type=jnp.float32)]
    ppermute x0 -> x48, starting transfers between devices: none -> 34.3 us  [the longest x42 28.7 us: swap(): return lax.ppermute(value, 'tp', [(i, i ^ d) for i in range(tp)])]
    psum x1 -> x0, blocking collectives: 29.7 us -> none  [shards(): squares = lax.psum(jnp.sum(local * local, axis=1), ('tp', 'sub'))]
    unnamed x9 -> x74, local copies, waits for them, and re-layouts: 7 us -> 33 us
  transfers between devices with their start and end apart: 3 -> 54, of which waited for: 3 -> 27; matrix products, arithmetic and copies ran while one was open for 1% -> 1% of each run, Pallas kernels for 0% -> 52%
where the time goes in v1:
time: 447 us; the launch traced here: 444 us
  Pallas kernels  234 us (52%)
  waiting for transfers between devices  124 us (28%)
  local copies, waits for them, and re-layouts  36.5 us (8%)
  starting transfers between devices  34.5 us (8%)
  between operations  14.4 us (3%)
    pallas_call x6, Pallas kernels, matmul_chunk(): pl.pallas_call(functools.partial(matmul_kernel, tp, len(after) + len(arri...  196 us
    ppermute x42, waiting for transfers between devices, swap(): return lax.ppermute(value, 'tp', [(i, i ^ d) for i in range(tp)])  88.8 us
    unnamed x74, local copies, waits for them, and re-layouts  33 us
    ppermute x42, starting transfers between devices, swap(): return lax.ppermute(value, 'tp', [(i, i ^ d) for i in range(tp)])  28.7 us
    all_gather x6, waiting for transfers between devices, shards(): gathered.append(lax.all_gather(own, 'sub', axis=0, tiled=True))  27.8 us
    pallas_call x6, Pallas kernels, norm_chunk(): pl.pallas_call(functools.partial(norm_kernel, tp, len(aliases) + len(afte...  16.1 us
    pallas_call x6, Pallas kernels, hidden_chunk(): pl.pallas_call(functools.partial(hidden_kernel, len(after)), grid=(1,), i...  12.2 us
    pallas_call x6, Pallas kernels, stream_chunk(): pl.pallas_call(functools.partial(stream_kernel, tp, len(aliases) + len(af...  9.31 us
  transfers between devices with their start and end apart: 54, of which 27 were waited for; matrix products, arithmetic and copies ran while one was open for 1% of the time, Pallas kernels for 52%

profile of v1, /device:TPU:0, one launch (start us, length us, event | category | flops | bytes accessed | tf_op | source)
XLA Modules:
  0.0 443.6 jit_solution(2905630913922028824)
XLA Ops:
  7.2 2.0 copy-done.1
  9.2 2.2 hidden_chunk.6
  11.5 1.9 copy-done.2
  13.4 2.2 hidden_chunk.7
  15.6 1.9 copy-done.3
  17.5 2.2 hidden_chunk.8
  19.7 2.1 copy-done.4
  21.8 2.2 hidden_chunk.9
  24.1 1.9 copy-done.5
  25.9 2.2 hidden_chunk.10
  28.2 1.9 copy-done.6
  32.4 27.8 %all-gather.17.cloned.1.call-done.piece = bf16[512,2048]{1,0:T(8,128)(2,1)} async-done(((bf16[128,2048]{1,0:T(8,128)(2,1)}), bf16[512,2048]{1,0:T(8,128)(2,1)}) %all-gather.17.cloned.1.call-update) | async-done | bytes 2097168 | tf_op jit(solution)/shard_map/all_gather | solution.py:274
  61.8 33.5 %matmul_chunk.6 = (f32[128,1024]{1,0:T(8,128)S(1)}, bf16[128,1024]{1,0:T(8,128)(2,1)}, bf16[128,1024]{1,0:T(8,128)(2,1)}, bf16[128,1024]{1,0:T(8,128)(2,1)}, f32[8,128]{1,0:T(8,128)S(1)}) custom-call(s32[2]{0:T(128)S(1)} %pad_add_fusion.where, bf16[512,2048]{1,0:T(8,128)(2,1)S(1)} %copy-done.12, bf16[8192,4096]{1,0:T(8,128)(2,1)} %weight.11, ...), custom_call_target="tpu_custom_call" | custom-call | flops 8589934592 | bytes 67108864 | tf_op jit(solution)/shard_map/matmul_chunk/pallas_call | solution.py:98
  98.7 2.8 gather_fusion
  101.6 3.9 collective-permute-done.1.refs_2_
  105.5 4.8 %collective-permute-done.2.refs_3_ = bf16[128,1024]{1,0:T(8,128)(2,1)} collective-permute-done((bf16[128,1024]{1,0:T(8,128)(2,1)}, bf16[128,1024]{1,0:T(8,128)(2,1)}, u32[]{:S(2)}, u32[]{:S(2)}) %collective-permute-start.2) | collective-permute-done | bytes 262176 | tf_op jit(solution)/shard_map/ppermute | solution.py:265
  111.4 2.3 stream_chunk.6
  115.5 32.4 %matmul_chunk.7 = (f32[128,1024]{1,0:T(8,128)S(1)}, bf16[128,1024]{1,0:T(8,128)(2,1)S(1)}, bf16[128,1024]{1,0:T(8,128)(2,1)S(1)}, bf16[128,1024]{1,0:T(8,128)(2,1)S(1)}, f32[8,128]{1,0:T(8,128)S(1)}) custom-call(s32[2]{0:T(128)S(1)} %pad_add_fusion.where, bf16[512,2048]{1,0:T(8,128)(2,1)S(1)} %copy-done.11, bf16[8192,4096]{1,0:T(8,128)(2,1)} %weight.11, ...), custom_call_target="tpu_custom_call" | custom-call | flops 8589934592 | bytes 67108864 | tf_op jit(solution)/shard_map/matmul_chunk/pallas_call | solution.py:98
  151.9 5.4 %collective-permute-done.4.refs_2_ = bf16[128,1024]{1,0:T(8,128)(2,1)S(1)} collective-permute-done((bf16[128,1024]{1,0:T(8,128)(2,1)S(1)}, bf16[128,1024]{1,0:T(8,128)(2,1)S(1)}, u32[]{:S(2)}, u32[]{:S(2)}) %collective-permute-start.4) | collective-permute-done | bytes 262176 | tf_op jit(solution)/shard_map/ppermute | solution.py:265
  157.3 4.7 %collective-permute-done.5.refs_3_ = bf16[128,1024]{1,0:T(8,128)(2,1)S(1)} collective-permute-done((bf16[128,1024]{1,0:T(8,128)(2,1)S(1)}, bf16[128,1024]{1,0:T(8,128)(2,1)S(1)}, u32[]{:S(2)}, u32[]{:S(2)}) %collective-permute-start.5) | collective-permute-done | bytes 262176 | tf_op jit(solution)/shard_map/ppermute | solution.py:265
  163.9 4.8 %collective-permute-done.7.refs_2_ = bf16[128,1024]{1,0:T(8,128)(2,1)} collective-permute-done((bf16[128,1024]{1,0:T(8,128)(2,1)}, bf16[128,1024]{1,0:T(8,128)(2,1)}, u32[]{:S(2)}, u32[]{:S(2)}) %collective-permute-start.7) | collective-permute-done | bytes 262176 | tf_op jit(solution)/shard_map/ppermute | solution.py:265
  168.7 4.4 collective-permute-done.8.refs_3_
  174.6 33.0 %matmul_chunk.8 = (f32[128,1024]{1,0:T(8,128)S(1)}, bf16[128,1024]{1,0:T(8,128)(2,1)S(1)}, bf16[128,1024]{1,0:T(8,128)(2,1)}, bf16[128,1024]{1,0:T(8,128)(2,1)S(1)}, f32[8,128]{1,0:T(8,128)S(1)}) custom-call(s32[2]{0:T(128)S(1)} %pad_add_fusion.where, bf16[512,2048]{1,0:T(8,128)(2,1)S(1)} %copy-done.10, bf16[8192,4096]{1,0:T(8,128)(2,1)} %weight.11, ...), custom_call_target="tpu_custom_call" | custom-call | flops 8589934592 | bytes 67108864 | tf_op jit(solution)/shard_map/matmul_chunk/pallas_call | solution.py:98
  213.5 5.2 %collective-permute-done.10.refs_2_ = bf16[128,1024]{1,0:T(8,128)(2,1)} collective-permute-done((bf16[128,1024]{1,0:T(8,128)(2,1)}, bf16[128,1024]{1,0:T(8,128)(2,1)}, u32[]{:S(2)}, u32[]{:S(2)}) %collective-permute-start.10) | collective-permute-done | bytes 262176 | tf_op jit(solution)/shard_map/ppermute | solution.py:265
  219.6 4.3 collective-permute-done.11.refs_3_
  224.9 2.2 stream_chunk.8
  227.1 2.8 collective-permute-done.13.refs_2_
  229.9 5.3 %collective-permute-done.14.refs_3_ = bf16[128,1024]{1,0:T(8,128)(2,1)} collective-permute-done((bf16[128,1024]{1,0:T(8,128)(2,1)}, bf16[128,1024]{1,0:T(8,128)(2,1)}, u32[]{:S(2)}, u32[]{:S(2)}) %collective-permute-start.14) | collective-permute-done | bytes 262176 | tf_op jit(solution)/shard_map/ppermute | solution.py:265
  236.8 32.6 %matmul_chunk.9 = (f32[128,1024]{1,0:T(8,128)S(1)}, bf16[128,1024]{1,0:T(8,128)(2,1)S(1)}, bf16[128,1024]{1,0:T(8,128)(2,1)S(1)}, bf16[128,1024]{1,0:T(8,128)(2,1)S(1)}, f32[8,128]{1,0:T(8,128)S(1)}) custom-call(s32[2]{0:T(128)S(1)} %pad_add_fusion.where, bf16[512,2048]{1,0:T(8,128)(2,1)S(1)} %copy-done.8, bf16[8192,4096]{1,0:T(8,128)(2,1)} %weight.11, ...), custom_call_target="tpu_custom_call" | custom-call | flops 8589934592 | bytes 67108864 | tf_op jit(solution)/shard_map/matmul_chunk/pallas_call | solution.py:98
  273.4 5.4 %collective-permute-done.16.refs_2_ = bf16[128,1024]{1,0:T(8,128)(2,1)S(1)} collective-permute-done((bf16[128,1024]{1,0:T(8,128)(2,1)S(1)}, bf16[128,1024]{1,0:T(8,128)(2,1)S(1)}, u32[]{:S(2)}, u32[]{:S(2)}) %collective-permute-start.16) | collective-permute-done | bytes 262176 | tf_op jit(solution)/shard_map/ppermute | solution.py:265
  278.9 4.7 %collective-permute-done.17.refs_3_ = bf16[128,1024]{1,0:T(8,128)(2,1)S(1)} collective-permute-done((bf16[128,1024]{1,0:T(8,128)(2,1)S(1)}, bf16[128,1024]{1,0:T(8,128)(2,1)S(1)}, u32[]{:S(2)}, u32[]{:S(2)}) %collective-permute-start.17) | collective-permute-done | bytes 262176 | tf_op jit(solution)/shard_map/ppermute | solution.py:265
  285.4 4.8 %collective-permute-done.19.refs_2_ = bf16[128,1024]{1,0:T(8,128)(2,1)} collective-permute-done((bf16[128,1024]{1,0:T(8,128)(2,1)}, bf16[128,1024]{1,0:T(8,128)(2,1)}, u32[]{:S(2)}, u32[]{:S(2)}) %collective-permute-start.19) | collective-permute-done | bytes 262176 | tf_op jit(solution)/shard_map/ppermute | solution.py:265
  290.2 4.2 collective-permute-done.20.refs_3_
  296.0 32.5 %matmul_chunk.10 = (f32[128,1024]{1,0:T(8,128)S(1)}, bf16[128,1024]{1,0:T(8,128)(2,1)S(1)}, bf16[128,1024]{1,0:T(8,128)(2,1)S(1)}, bf16[128,1024]{1,0:T(8,128)(2,1)S(1)}, f32[8,128]{1,0:T(8,128)S(1)}) custom-call(s32[2]{0:T(128)S(1)} %pad_add_fusion.where, bf16[512,2048]{1,0:T(8,128)(2,1)S(1)} %copy-done.7, bf16[8192,4096]{1,0:T(8,128)(2,1)} %weight.11, ...), custom_call_target="tpu_custom_call" | custom-call | flops 8589934592 | bytes 67108864 | tf_op jit(solution)/shard_map/matmul_chunk/pallas_call | solution.py:98
  332.8 5.5 %collective-permute-done.22.refs_2_ = bf16[128,1024]{1,0:T(8,128)(2,1)S(1)} collective-permute-done((bf16[128,1024]{1,0:T(8,128)(2,1)S(1)}, bf16[128,1024]{1,0:T(8,128)(2,1)S(1)}, u32[]{:S(2)}, u32[]{:S(2)}) %collective-permute-start.22) | collective-permute-done | bytes 262176 | tf_op jit(solution)/shard_map/ppermute | solution.py:265
  338.2 4.7 %collective-permute-done.23.refs_3_ = bf16[128,1024]{1,0:T(8,128)(2,1)S(1)} collective-permute-done((bf16[128,1024]{1,0:T(8,128)(2,1)S(1)}, bf16[128,1024]{1,0:T(8,128)(2,1)S(1)}, u32[]{:S(2)}, u32[]{:S(2)}) %collective-permute-start.23) | collective-permute-done | bytes 262176 | tf_op jit(solution)/shard_map/ppermute | solution.py:265
  346.6 2.3 collective-permute-start.35
  350.2 3.2 collective-permute-done.26.refs_3_
  360.1 32.3 %matmul_chunk.11 = (f32[128,1024]{1,0:T(8,128)S(1)}, bf16[128,1024]{1,0:T(8,128)(2,1)S(1)}, bf16[128,1024]{1,0:T(8,128)(2,1)S(1)}, bf16[128,1024]{1,0:T(8,128)(2,1)S(1)}, f32[8,128]{1,0:T(8,128)S(1)}) custom-call(s32[2]{0:T(128)S(1)} %pad_add_fusion.where, bf16[512,2048]{1,0:T(8,128)(2,1)S(1)} %copy-done.9, bf16[8192,4096]{1,0:T(8,128)(2,1)} %weight.11, ...), custom_call_target="tpu_custom_call" | custom-call | flops 8589934592 | bytes 67108864 | tf_op jit(solution)/shard_map/matmul_chunk/pallas_call | solution.py:98
  394.8 6.5 %collective-permute-done.38 = f32[8,640]{1,0:T(8,128)S(1)} collective-permute-done((f32[8,640]{1,0:T(8,128)S(1)}, f32[8,640]{1,0:T(8,128)S(1)}, u32[]{:S(2)}, u32[]{:S(2)}) %collective-permute-start.38) | collective-permute-done | bytes 20512 | tf_op jit(solution)/shard_map/ppermute | solution.py:265
  404.4 3.1 norm_chunk.6
  407.4 3.0 norm_chunk.7
  410.4 3.1 norm_chunk.8
  413.5 1.9 norm_chunk.9
  415.5 3.1 norm_chunk.10
  423.2 3.8 collective-permute-done.42
  427.0 3.6 collective-permute-done.44
  434.8 1.9 norm_chunk.11
  (176 shorter events, 65.1 us)
Async XLA Ops:
  7.2 53.0 %all-gather.17.cloned.1.call-start = ((), (), s32[]{:S(2)}) async-start(), calls=%async_computation.5 | async-start | bytes 2621440 | tf_op jit(solution)/shard_map/all_gather | solution.py:274
  11.4 102.3 %all-gather.15.cloned.1.call-start = ((), (), s32[]{:S(2)}) async-start(), calls=%async_computation.4 | async-start | bytes 2621440 | tf_op jit(solution)/shard_map/all_gather | solution.py:274
  15.6 148.3 %all-gather.13.cloned.1.call-start = ((), (), s32[]{:S(2)}) async-start(), calls=%async_computation.3 | async-start | bytes 2621440 | tf_op jit(solution)/shard_map/all_gather | solution.py:274
  19.7 207.4 %all-gather.11.cloned.1.call-start = ((), (), s32[]{:S(2)}) async-start(), calls=%async_computation.2 | async-start | bytes 2621440 | tf_op jit(solution)/shard_map/all_gather | solution.py:274
  24.0 261.4 %all-gather.9.cloned.1.call-start = ((), (), s32[]{:S(2)}) async-start(), calls=%async_computation.1 | async-start | bytes 2621440 | tf_op jit(solution)/shard_map/all_gather | solution.py:274
  28.2 327.5 %all-gather.7.cloned.1.call-start = ((), (), s32[]{:S(2)}) async-start(), calls=%async_computation | async-start | bytes 2621440 | tf_op jit(solution)/shard_map/all_gather | solution.py:274
  96.1 5.5 %collective-permute-start = (bf16[128,1024]{1,0:T(8,128)(2,1)}, bf16[128,1024]{1,0:T(8,128)(2,1)S(1)}, u32[]{:S(2)}, u32[]{:S(2)}) collective-permute-start(bf16[128,1024]{1,0:T(8,128)(2,1)} %get-tuple-element.86), channel_id=1, source_target_pairs={{0,4},{4,0},{8,12},{12,8},{1,5},{5,1},{9,13},{13,9},{2,6},{6,2},{1... | collective-permute-start | bytes 786440 | tf_op jit(solution)/shard_map/ppermute | solution.py:265
  96.1 9.4 %collective-permute-start.1 = (bf16[128,1024]{1,0:T(8,128)(2,1)}, bf16[128,1024]{1,0:T(8,128)(2,1)}, u32[]{:S(2)}, u32[]{:S(2)}) collective-permute-start(bf16[128,1024]{1,0:T(8,128)(2,1)} %get-tuple-element.87), channel_id=1, source_target_pairs={{0,8},{4,12},{8,0},{12,4},{1,9},{5,13},{9,1},{13,5},{2,10},{6,14},... | collective-permute-start | bytes 786440 | tf_op jit(solution)/shard_map/ppermute | solution.py:265
  97.6 12.8 %collective-permute-start.2 = (bf16[128,1024]{1,0:T(8,128)(2,1)}, bf16[128,1024]{1,0:T(8,128)(2,1)}, u32[]{:S(2)}, u32[]{:S(2)}) collective-permute-start(bf16[128,1024]{1,0:T(8,128)(2,1)} %get-tuple-element.88), channel_id=1, source_target_pairs={{0,12},{4,8},{8,4},{12,0},{1,13},{5,9},{9,5},{13,1},{2,14},{6,10},... | collective-permute-start | bytes 786440 | tf_op jit(solution)/shard_map/ppermute | solution.py:265
  148.2 9.1 %collective-permute-start.4 = (bf16[128,1024]{1,0:T(8,128)(2,1)S(1)}, bf16[128,1024]{1,0:T(8,128)(2,1)S(1)}, u32[]{:S(2)}, u32[]{:S(2)}) collective-permute-start(bf16[128,1024]{1,0:T(8,128)(2,1)S(1)} %get-tuple-element.93), channel_id=1, source_target_pairs={{0,8},{4,12},{8,0},{12,4},{1,9},{5,13},{9,1},{13,5},{2,10},{6,14},... | collective-permute-start | bytes 786440 | tf_op jit(solution)/shard_map/ppermute | solution.py:265
  149.7 12.3 %collective-permute-start.5 = (bf16[128,1024]{1,0:T(8,128)(2,1)S(1)}, bf16[128,1024]{1,0:T(8,128)(2,1)S(1)}, u32[]{:S(2)}, u32[]{:S(2)}) collective-permute-start(bf16[128,1024]{1,0:T(8,128)(2,1)S(1)} %get-tuple-element.94), channel_id=1, source_target_pairs={{0,12},{4,8},{8,4},{12,0},{1,13},{5,9},{9,5},{13,1},{2,14},{6,10},... | collective-permute-start | bytes 786440 | tf_op jit(solution)/shard_map/ppermute | solution.py:265
  149.8 14.0 %collective-permute-start.6 = (bf16[128,1024]{1,0:T(8,128)(2,1)}, bf16[128,1024]{1,0:T(8,128)(2,1)S(1)}, u32[]{:S(2)}, u32[]{:S(2)}) collective-permute-start(bf16[128,1024]{1,0:T(8,128)(2,1)} %get-tuple-element.98.refs_0_), channel_id=1, source_target_pairs={{0,4},{4,0},{8,12},{12,8},{1,5},{5,1},{9,13},{13,9},{2,6},{6,2},{1... | collective-permute-start | bytes 786440 | tf_op jit(solution)/shard_map/ppermute | solution.py:265
  150.3 18.3 %collective-permute-start.7 = (bf16[128,1024]{1,0:T(8,128)(2,1)}, bf16[128,1024]{1,0:T(8,128)(2,1)}, u32[]{:S(2)}, u32[]{:S(2)}) collective-permute-start(bf16[128,1024]{1,0:T(8,128)(2,1)} %get-tuple-element.98.refs_0_), channel_id=1, source_target_pairs={{0,8},{4,12},{8,0},{12,4},{1,9},{5,13},{9,1},{13,5},{2,10},{6,14},... | collective-permute-start | bytes 786440 | tf_op jit(solution)/shard_map/ppermute | solution.py:265
  151.9 21.1 %collective-permute-start.8 = (bf16[128,1024]{1,0:T(8,128)(2,1)}, bf16[128,1024]{1,0:T(8,128)(2,1)}, u32[]{:S(2)}, u32[]{:S(2)}) collective-permute-start(bf16[128,1024]{1,0:T(8,128)(2,1)} %get-tuple-element.98.refs_0_), channel_id=1, source_target_pairs={{0,12},{4,8},{8,4},{12,0},{1,13},{5,9},{9,5},{13,1},{2,14},{6,10},... | collective-permute-start | bytes 786440 | tf_op jit(solution)/shard_map/ppermute | solution.py:265
  209.2 9.5 %collective-permute-start.10 = (bf16[128,1024]{1,0:T(8,128)(2,1)}, bf16[128,1024]{1,0:T(8,128)(2,1)}, u32[]{:S(2)}, u32[]{:S(2)}) collective-permute-start(bf16[128,1024]{1,0:T(8,128)(2,1)} %get-tuple-element.101), channel_id=1, source_target_pairs={{0,8},{4,12},{8,0},{12,4},{1,9},{5,13},{9,1},{13,5},{2,10},{6,14},... | collective-permute-start | bytes 786440 | tf_op jit(solution)/shard_map/ppermute | solution.py:265
  210.8 13.1 %collective-permute-start.11 = (bf16[128,1024]{1,0:T(8,128)(2,1)}, bf16[128,1024]{1,0:T(8,128)(2,1)S(1)}, u32[]{:S(2)}, u32[]{:S(2)}) collective-permute-start(bf16[128,1024]{1,0:T(8,128)(2,1)} %copy-done.33), channel_id=1, source_target_pairs={{0,12},{4,8},{8,4},{12,0},{1,13},{5,9},{9,5},{13,1},{2,14},{6,10},... | collective-permute-start | bytes 786440 | tf_op jit(solution)/shard_map/ppermute | solution.py:265
  211.4 12.4 %collective-permute-start.9 = (bf16[128,1024]{1,0:T(8,128)(2,1)}, bf16[128,1024]{1,0:T(8,128)(2,1)S(1)}, u32[]{:S(2)}, u32[]{:S(2)}) collective-permute-start(bf16[128,1024]{1,0:T(8,128)(2,1)} %copy-done.32), channel_id=1, source_target_pairs={{0,4},{4,0},{8,12},{12,8},{1,5},{5,1},{9,13},{13,9},{2,6},{6,2},{1... | collective-permute-start | bytes 786440 | tf_op jit(solution)/shard_map/ppermute | solution.py:265
  211.4 15.7 %collective-permute-start.12 = (bf16[128,1024]{1,0:T(8,128)(2,1)}, bf16[128,1024]{1,0:T(8,128)(2,1)S(1)}, u32[]{:S(2)}, u32[]{:S(2)}) collective-permute-start(bf16[128,1024]{1,0:T(8,128)(2,1)} %copy-done.27), channel_id=1, source_target_pairs={{0,4},{4,0},{8,12},{12,8},{1,5},{5,1},{9,13},{13,9},{2,6},{6,2},{1... | collective-permute-start | bytes 786440 | tf_op jit(solution)/shard_map/ppermute | solution.py:265
  211.9 18.0 %collective-permute-start.13 = (bf16[128,1024]{1,0:T(8,128)(2,1)}, bf16[128,1024]{1,0:T(8,128)(2,1)}, u32[]{:S(2)}, u32[]{:S(2)}) collective-permute-start(bf16[128,1024]{1,0:T(8,128)(2,1)} %copy-done.27), channel_id=1, source_target_pairs={{0,8},{4,12},{8,0},{12,4},{1,9},{5,13},{9,1},{13,5},{2,10},{6,14},... | collective-permute-start | bytes 786440 | tf_op jit(solution)/shard_map/ppermute | solution.py:265
  218.7 16.5 %collective-permute-start.14 = (bf16[128,1024]{1,0:T(8,128)(2,1)}, bf16[128,1024]{1,0:T(8,128)(2,1)}, u32[]{:S(2)}, u32[]{:S(2)}) collective-permute-start(bf16[128,1024]{1,0:T(8,128)(2,1)} %copy-done.27), channel_id=1, source_target_pairs={{0,12},{4,8},{8,4},{12,0},{1,13},{5,9},{9,5},{13,1},{2,14},{6,10},... | collective-permute-start | bytes 786440 | tf_op jit(solution)/shard_map/ppermute | solution.py:265
  269.4 4.0 collective-permute-start.15
  269.7 9.1 %collective-permute-start.16 = (bf16[128,1024]{1,0:T(8,128)(2,1)S(1)}, bf16[128,1024]{1,0:T(8,128)(2,1)S(1)}, u32[]{:S(2)}, u32[]{:S(2)}) collective-permute-start(bf16[128,1024]{1,0:T(8,128)(2,1)S(1)} %get-tuple-element.109), channel_id=1, source_target_pairs={{0,8},{4,12},{8,0},{12,4},{1,9},{5,13},{9,1},{13,5},{2,10},{6,14},... | collective-permute-start | bytes 786440 | tf_op jit(solution)/shard_map/ppermute | solution.py:265
  271.3 12.3 %collective-permute-start.17 = (bf16[128,1024]{1,0:T(8,128)(2,1)S(1)}, bf16[128,1024]{1,0:T(8,128)(2,1)S(1)}, u32[]{:S(2)}, u32[]{:S(2)}) collective-permute-start(bf16[128,1024]{1,0:T(8,128)(2,1)S(1)} %get-tuple-element.110), channel_id=1, source_target_pairs={{0,12},{4,8},{8,4},{12,0},{1,13},{5,9},{9,5},{13,1},{2,14},{6,10},... | collective-permute-start | bytes 786440 | tf_op jit(solution)/shard_map/ppermute | solution.py:265
  271.3 14.1 %collective-permute-start.18 = (bf16[128,1024]{1,0:T(8,128)(2,1)}, bf16[128,1024]{1,0:T(8,128)(2,1)}, u32[]{:S(2)}, u32[]{:S(2)}) collective-permute-start(bf16[128,1024]{1,0:T(8,128)(2,1)} %get-tuple-element.114.refs_0_), channel_id=1, source_target_pairs={{0,4},{4,0},{8,12},{12,8},{1,5},{5,1},{9,13},{13,9},{2,6},{6,2},{1... | collective-permute-start | bytes 786440 | tf_op jit(solution)/shard_map/ppermute | solution.py:265
  271.9 18.3 %collective-permute-start.19 = (bf16[128,1024]{1,0:T(8,128)(2,1)}, bf16[128,1024]{1,0:T(8,128)(2,1)}, u32[]{:S(2)}, u32[]{:S(2)}) collective-permute-start(bf16[128,1024]{1,0:T(8,128)(2,1)} %get-tuple-element.114.refs_0_), channel_id=1, source_target_pairs={{0,8},{4,12},{8,0},{12,4},{1,9},{5,13},{9,1},{13,5},{2,10},{6,14},... | collective-permute-start | bytes 786440 | tf_op jit(solution)/shard_map/ppermute | solution.py:265
  273.4 21.0 %collective-permute-start.20 = (bf16[128,1024]{1,0:T(8,128)(2,1)}, bf16[128,1024]{1,0:T(8,128)(2,1)}, u32[]{:S(2)}, u32[]{:S(2)}) collective-permute-start(bf16[128,1024]{1,0:T(8,128)(2,1)} %get-tuple-element.114.refs_0_), channel_id=1, source_target_pairs={{0,12},{4,8},{8,4},{12,0},{1,13},{5,9},{9,5},{13,1},{2,14},{6,10},... | collective-permute-start | bytes 786440 | tf_op jit(solution)/shard_map/ppermute | solution.py:265
  328.5 4.3 collective-permute-start.21
  329.1 9.2 %collective-permute-start.22 = (bf16[128,1024]{1,0:T(8,128)(2,1)S(1)}, bf16[128,1024]{1,0:T(8,128)(2,1)S(1)}, u32[]{:S(2)}, u32[]{:S(2)}) collective-permute-start(bf16[128,1024]{1,0:T(8,128)(2,1)S(1)} %get-tuple-element.117), channel_id=1, source_target_pairs={{0,8},{4,12},{8,0},{12,4},{1,9},{5,13},{9,1},{13,5},{2,10},{6,14},... | collective-permute-start | bytes 786440 | tf_op jit(solution)/shard_map/ppermute | solution.py:265
  330.6 12.3 %collective-permute-start.23 = (bf16[128,1024]{1,0:T(8,128)(2,1)S(1)}, bf16[128,1024]{1,0:T(8,128)(2,1)S(1)}, u32[]{:S(2)}, u32[]{:S(2)}) collective-permute-start(bf16[128,1024]{1,0:T(8,128)(2,1)S(1)} %get-tuple-element.118), channel_id=1, source_target_pairs={{0,12},{4,8},{8,4},{12,0},{1,13},{5,9},{9,5},{13,1},{2,14},{6,10},... | collective-permute-start | bytes 786440 | tf_op jit(solution)/shard_map/ppermute | solution.py:265
  330.6 15.2 %collective-permute-start.24 = (bf16[128,1024]{1,0:T(8,128)(2,1)S(1)}, bf16[128,1024]{1,0:T(8,128)(2,1)S(1)}, u32[]{:S(2)}, u32[]{:S(2)}) collective-permute-start(bf16[128,1024]{1,0:T(8,128)(2,1)S(1)} %copy-done.30), channel_id=1, source_target_pairs={{0,4},{4,0},{8,12},{12,8},{1,5},{5,1},{9,13},{13,9},{2,6},{6,2},{1... | collective-permute-start | bytes 786440 | tf_op jit(solution)/shard_map/ppermute | solution.py:265
  331.2 18.2 %collective-permute-start.25 = (bf16[128,1024]{1,0:T(8,128)(2,1)S(1)}, bf16[128,1024]{1,0:T(8,128)(2,1)S(1)}, u32[]{:S(2)}, u32[]{:S(2)}) collective-permute-start(bf16[128,1024]{1,0:T(8,128)(2,1)S(1)} %copy-done.30), channel_id=1, source_target_pairs={{0,8},{4,12},{8,0},{12,4},{1,9},{5,13},{9,1},{13,5},{2,10},{6,14},... | collective-permute-start | bytes 786440 | tf_op jit(solution)/shard_map/ppermute | solution.py:265
  332.8 20.6 %collective-permute-start.26 = (bf16[128,1024]{1,0:T(8,128)(2,1)S(1)}, bf16[128,1024]{1,0:T(8,128)(2,1)S(1)}, u32[]{:S(2)}, u32[]{:S(2)}) collective-permute-start(bf16[128,1024]{1,0:T(8,128)(2,1)S(1)} %copy-done.30), channel_id=1, source_target_pairs={{0,12},{4,8},{8,4},{12,0},{1,13},{5,9},{9,5},{13,1},{2,14},{6,10},... | collective-permute-start | bytes 786440 | tf_op jit(solution)/shard_map/ppermute | solution.py:265
  344.2 48.2 %collective-permute-start.33 = (f32[8,640]{1,0:T(8,128)S(1)}, f32[8,640]{1,0:T(8,128)S(1)}, u32[]{:S(2)}, u32[]{:S(2)}) collective-permute-start(f32[8,640]{1,0:T(8,128)S(1)} %constant_dynamic-update-slice_fusion), channel_id=1, source_target_pairs={{0,1},{1,2},{2,3},{3,0},{4,5},{5,6},{6,7},{7,4},{8,9},{9,10},{10,1... | collective-permute-start | bytes 61448 | tf_op jit(solution)/shard_map/ppermute | solution.py:282
  344.2 48.8 %collective-permute-start.34 = (f32[8,640]{1,0:T(8,128)S(1)}, f32[8,640]{1,0:T(8,128)S(1)}, u32[]{:S(2)}, u32[]{:S(2)}) collective-permute-start(f32[8,640]{1,0:T(8,128)S(1)} %constant_dynamic-update-slice_fusion), channel_id=1, source_target_pairs={{0,2},{1,3},{2,0},{3,1},{4,6},{5,7},{6,4},{7,5},{8,10},{9,11},{10,... | collective-permute-start | bytes 61448 | tf_op jit(solution)/shard_map/ppermute | solution.py:282
  346.6 46.5 %collective-permute-start.35 = (f32[8,640]{1,0:T(8,128)S(1)}, f32[8,640]{1,0:T(8,128)S(1)}, u32[]{:S(2)}, u32[]{:S(2)}) collective-permute-start(f32[8,640]{1,0:T(8,128)S(1)} %constant_dynamic-update-slice_fusion), channel_id=1, source_target_pairs={{0,3},{1,0},{2,1},{3,2},{4,7},{5,4},{6,5},{7,6},{8,11},{9,8},{10,9... | collective-permute-start | bytes 61448 | tf_op jit(solution)/shard_map/ppermute | solution.py:282
  350.2 52.9 %collective-permute-start.30 = (bf16[128,1024]{1,0:T(8,128)(2,1)}, bf16[128,1024]{1,0:T(8,128)(2,1)}, u32[]{:S(2)}, u32[]{:S(2)}) collective-permute-start(bf16[128,1024]{1,0:T(8,128)(2,1)} %get-tuple-element.128.refs_0_), channel_id=1, source_target_pairs={{0,4},{4,0},{8,12},{12,8},{1,5},{5,1},{9,13},{13,9},{2,6},{6,2},{1... | collective-permute-start | bytes 786440 | tf_op jit(solution)/shard_map/ppermute | solution.py:265
  354.1 61.4 %collective-permute-start.31 = (bf16[128,1024]{1,0:T(8,128)(2,1)}, bf16[128,1024]{1,0:T(8,128)(2,1)}, u32[]{:S(2)}, u32[]{:S(2)}) collective-permute-start(bf16[128,1024]{1,0:T(8,128)(2,1)} %get-tuple-element.128.refs_0_), channel_id=1, source_target_pairs={{0,8},{4,12},{8,0},{12,4},{1,9},{5,13},{9,1},{13,5},{2,10},{6,14},... | collective-permute-start | bytes 786440 | tf_op jit(solution)/shard_map/ppermute | solution.py:265
  392.4 23.1 %collective-permute-start.32 = (bf16[128,1024]{1,0:T(8,128)(2,1)}, bf16[128,1024]{1,0:T(8,128)(2,1)S(1)}, u32[]{:S(2)}, u32[]{:S(2)}) collective-permute-start(bf16[128,1024]{1,0:T(8,128)(2,1)} %get-tuple-element.128.refs_0_), channel_id=1, source_target_pairs={{0,12},{4,8},{8,4},{12,0},{1,13},{5,9},{9,5},{13,1},{2,14},{6,10},... | collective-permute-start | bytes 786440 | tf_op jit(solution)/shard_map/ppermute | solution.py:265
  393.0 8.3 %collective-permute-start.38 = (f32[8,640]{1,0:T(8,128)S(1)}, f32[8,640]{1,0:T(8,128)S(1)}, u32[]{:S(2)}, u32[]{:S(2)}) collective-permute-start(f32[8,640]{1,0:T(8,128)S(1)} %add_add_fusion), channel_id=1, source_target_pairs={{0,12},{4,8},{8,4},{12,0},{1,13},{5,9},{9,5},{13,1},{2,14},{6,10},... | collective-permute-start | bytes 61448 | tf_op jit(solution)/shard_map/ppermute | solution.py:265
  394.3 7.9 %collective-permute-start.37 = (f32[8,640]{1,0:T(8,128)S(1)}, f32[8,640]{1,0:T(8,128)S(1)}, u32[]{:S(2)}, u32[]{:S(2)}) collective-permute-start(f32[8,640]{1,0:T(8,128)S(1)} %add_add_fusion), channel_id=1, source_target_pairs={{0,8},{4,12},{8,0},{12,4},{1,9},{5,13},{9,1},{13,5},{2,10},{6,14},... | collective-permute-start | bytes 61448 | tf_op jit(solution)/shard_map/ppermute | solution.py:265
  402.2 16.3 %collective-permute-start.27 = (bf16[128,1024]{1,0:T(8,128)(2,1)S(1)}, bf16[128,1024]{1,0:T(8,128)(2,1)S(1)}, u32[]{:S(2)}, u32[]{:S(2)}) collective-permute-start(bf16[128,1024]{1,0:T(8,128)(2,1)S(1)} %get-tuple-element.124), channel_id=1, source_target_pairs={{0,4},{4,0},{8,12},{12,8},{1,5},{5,1},{9,13},{13,9},{2,6},{6,2},{1... | collective-permute-start | bytes 786440 | tf_op jit(solution)/shard_map/ppermute | solution.py:265
  402.6 15.9 %collective-permute-start.28 = (bf16[128,1024]{1,0:T(8,128)(2,1)S(1)}, bf16[128,1024]{1,0:T(8,128)(2,1)S(1)}, u32[]{:S(2)}, u32[]{:S(2)}) collective-permute-start(bf16[128,1024]{1,0:T(8,128)(2,1)S(1)} %get-tuple-element.125), channel_id=1, source_target_pairs={{0,8},{4,12},{8,0},{12,4},{1,9},{5,13},{9,1},{13,5},{2,10},{6,14},... | collective-permute-start | bytes 786440 | tf_op jit(solution)/shard_map/ppermute | solution.py:265
  403.1 15.4 %collective-permute-start.29 = (bf16[128,1024]{1,0:T(8,128)(2,1)S(1)}, bf16[128,1024]{1,0:T(8,128)(2,1)S(1)}, u32[]{:S(2)}, u32[]{:S(2)}) collective-permute-start(bf16[128,1024]{1,0:T(8,128)(2,1)S(1)} %get-tuple-element.126), channel_id=1, source_target_pairs={{0,12},{4,8},{8,4},{12,0},{1,13},{5,9},{9,5},{13,1},{2,14},{6,10},... | collective-permute-start | bytes 786440 | tf_op jit(solution)/shard_map/ppermute | solution.py:265
  419.7 15.1 %collective-permute-start.39 = (bf16[128,1024]{1,0:T(8,128)(2,1)S(1)}, bf16[128,1024]{1,0:T(8,128)(2,1)S(1)}, u32[]{:S(2)}, u32[]{:S(2)}) collective-permute-start(bf16[128,1024]{1,0:T(8,128)(2,1)S(1)} %get-tuple-element.140.refs_0_), channel_id=1, source_target_pairs={{0,4},{4,0},{8,12},{12,8},{1,5},{5,1},{9,13},{13,9},{2,6},{6,2},{1... | collective-permute-start | bytes 786440 | tf_op jit(solution)/shard_map/ppermute | solution.py:265
  420.2 14.6 %collective-permute-start.40 = (bf16[128,1024]{1,0:T(8,128)(2,1)S(1)}, bf16[128,1024]{1,0:T(8,128)(2,1)S(1)}, u32[]{:S(2)}, u32[]{:S(2)}) collective-permute-start(bf16[128,1024]{1,0:T(8,128)(2,1)S(1)} %get-tuple-element.140.refs_0_), channel_id=1, source_target_pairs={{0,8},{4,12},{8,0},{12,4},{1,9},{5,13},{9,1},{13,5},{2,10},{6,14},... | collective-permute-start | bytes 786440 | tf_op jit(solution)/shard_map/ppermute | solution.py:265
  420.6 14.2 %collective-permute-start.41 = (bf16[128,1024]{1,0:T(8,128)(2,1)S(1)}, bf16[128,1024]{1,0:T(8,128)(2,1)S(1)}, u32[]{:S(2)}, u32[]{:S(2)}) collective-permute-start(bf16[128,1024]{1,0:T(8,128)(2,1)S(1)} %get-tuple-element.140.refs_0_), channel_id=1, source_target_pairs={{0,12},{4,8},{8,4},{12,0},{1,13},{5,9},{9,5},{13,1},{2,14},{6,10},... | collective-permute-start | bytes 786440 | tf_op jit(solution)/shard_map/ppermute | solution.py:265
  421.6 5.4 %collective-permute-start.42 = (f32[8,128]{1,0:T(8,128)S(1)}, f32[8,128]{1,0:T(8,128)S(1)}, u32[]{:S(2)}, u32[]{:S(2)}) collective-permute-start(f32[8,128]{1,0:T(8,128)S(1)} %get-tuple-element.141), channel_id=1, source_target_pairs={{0,1},{1,2},{2,3},{3,0},{4,5},{5,6},{6,7},{7,4},{8,9},{9,10},{10,1... | collective-permute-start | bytes 12296 | tf_op jit(solution)/shard_map/ppermute | solution.py:282
  421.6 5.4 %collective-permute-start.43 = (f32[8,128]{1,0:T(8,128)S(1)}, f32[8,128]{1,0:T(8,128)S(1)}, u32[]{:S(2)}, u32[]{:S(2)}) collective-permute-start(f32[8,128]{1,0:T(8,128)S(1)} %get-tuple-element.141), channel_id=1, source_target_pairs={{0,2},{1,3},{2,0},{3,1},{4,6},{5,7},{6,4},{7,5},{8,10},{9,11},{10,... | collective-permute-start | bytes 12296 | tf_op jit(solution)/shard_map/ppermute | solution.py:282
  (41 other events, 397.9 us)
Sparse Core Ops, SparseCore 0:
  11.5 48.6 all-gather.16
  62.4 44.8 all-gather.14
  108.8 44.4 all-gather.12
  154.7 44.8 all-gather.10
  201.1 44.8 all-gather.8
  247.3 44.6 all-gather.6
